TPU v7x, 512 devices: a whole 4x8x8 slice. The times are simulated.
512 devices in a mesh: grp: 4 (over x), comp: 128 (over y, z, core).
Axes of the slice: x: 4, y: 8, z: 8, core: 2. Of those that a mesh axis runs over, the one named last changes fastest.
Arguments:
- spectra: float32 [600, 196608], P('grp', 'comp'), may hold values from 0.05 to 2
- wind_speed: float32 [196608], P('comp'), may hold values from 4 to 24
- wind_dir: float32 [196608], P('comp'), may hold values from -3.140625 to 3.140625
- sea_cell: int32 [196608], P('comp'), may hold values from 0 to 2047, as said below
Outputs:
- spectra_grid: float32 [600, 1024, 256], P('grp', 'comp')
Inputs may be any that keep to these rules, and one draw needn't show every extreme that they name: `sea_cell`: each aligned block of 1536 entries names 1536 different cells of one tile of 8 x 256 cells (row * 256 + column).
All inputs are finite; a program needn't handle non-finite values.
Results may differ from a plain program's by a relative error of at most 0.0003.
Values sent between devices are 32-bit elements; how exact they have to be, the bound alone decides.
No kernel may reach another device: no remote copies, remote signals or barrier semaphores. Data moves between devices by JAX's collectives and lax.ppermute only.
A program may use at most 64 MiB of HBM per device.

v0:
```python
import math
import jax
import jax.numpy as jnp
from jax import lax
from jax.sharding import PartitionSpec as P

FREQ = 25
TROWS = 8
NY = 256
ADV_STEPS = 2
GRAV = 9.81
LOW_FREQ = 0.0418
FREQ_STEP = 1.1


def padded_2(block, sides, width):
    for axis, dim in sides:
        count = lax.axis_size(axis)
        forward = [(i, i + 1) for i in range(count - 1)]
        backward = [(target, source) for source, target in forward]
        low = lax.ppermute(
            lax.slice_in_dim(block, block.shape[dim] - width, None, axis=dim), axis, forward
        )
        high = lax.ppermute(lax.slice_in_dim(block, 0, width, axis=dim), axis, backward)
        block = jnp.concatenate([low, block, high], axis=dim)
    return block


def spectral_tables(first_dir, dir_count, total_dirs, freq_count):
    component = jnp.arange(dir_count * freq_count, dtype=jnp.int32)
    direction = (component // freq_count + first_dir).astype(jnp.float32)
    frequency = LOW_FREQ * jnp.power(
        jnp.float32(FREQ_STEP), (component % freq_count).astype(jnp.float32)
    )
    angles = 2.0 * math.pi * (direction + 0.5) / total_dirs
    angular = 2.0 * math.pi * frequency
    weight = 2.0 * math.pi / total_dirs * 0.1 * frequency
    return (angles, angular, weight)


def source_terms(spectra, energy, inverse, angles, angular, wind_speed, wind_dir):
    mean_freq = energy / inverse
    wavenumber = mean_freq * mean_freq / GRAV
    steepness = energy * wavenumber * wavenumber
    steep_ratio = steepness / (steepness + 0.02)
    forcing = 28.0 * 0.035 * wind_speed * jnp.cos(angles - wind_dir) * angular / GRAV
    rate_in = 0.1 * jnp.maximum(forcing - 1.0, 0.0)
    relative = angular / mean_freq
    rate_out = 0.4 * relative * relative * steep_ratio
    return spectra * jnp.exp(rate_in - rate_out)


def courant(angles, angular):
    reach = 0.45 * (2.0 * math.pi * LOW_FREQ) / angular
    return (reach * jnp.cos(angles), reach * jnp.sin(angles))


def koren_slope(slope_back, slope_ahead):
    middle = (slope_back + 2.0 * slope_ahead) / 3.0
    rising = jnp.maximum(0.0, jnp.minimum(jnp.minimum(2.0 * slope_ahead, middle), 2.0 * slope_back))
    falling = jnp.minimum(
        0.0, jnp.maximum(jnp.maximum(2.0 * slope_ahead, middle), 2.0 * slope_back)
    )
    return jnp.where(slope_back >= 0.0, rising, falling)


def face_flux(back_one, centre, ahead_one, ahead_two, number):
    forward = number >= 0.0
    upstream = jnp.where(forward, centre, ahead_one)
    slope_back = jnp.where(forward, centre - back_one, ahead_one - ahead_two)
    slope_ahead = jnp.where(forward, ahead_one - centre, centre - ahead_one)
    return number * (
        upstream + 0.5 * (1.0 - jnp.abs(number)) * koren_slope(slope_back, slope_ahead)
    )


def advect(padded, courant_x, courant_y):
    count = padded.shape[-2] - 4
    flux_rows = face_flux(
        padded[..., 0 : count + 1, :],
        padded[..., 1 : count + 2, :],
        padded[..., 2 : count + 3, :],
        padded[..., 3 : count + 4, :],
        courant_x,
    )
    centre = padded[..., 2 : count + 2, :]
    flux_cols = face_flux(
        jnp.roll(centre, 1, -1),
        centre,
        jnp.roll(centre, -1, -1),
        jnp.roll(centre, -2, -1),
        courant_y,
    )
    return (
        centre
        - (flux_rows[..., 1:, :] - flux_rows[..., :-1, :])
        - (flux_cols - jnp.roll(flux_cols, 1, -1))
    )


def local(spectra, wind_speed, wind_dir, sea_cell):
    local_comps = spectra.shape[0]
    dir_count = local_comps // FREQ
    group_index = lax.axis_index("grp")
    angles, angular, weight = spectral_tables(
        group_index * dir_count, dir_count, dir_count * lax.axis_size("grp"), FREQ
    )
    partial_energy = jnp.sum(weight[:, None] * spectra, axis=0)
    partial_inverse = jnp.sum((weight / angular)[:, None] * spectra, axis=0)
    energy, inverse = lax.psum((partial_energy, partial_inverse), "grp")
    sourced = source_terms(
        spectra,
        energy,
        inverse,
        angles[:, None],
        angular[:, None],
        wind_speed[None, :],
        wind_dir[None, :],
    )
    received = lax.all_to_all(sourced, "comp", split_axis=1, concat_axis=1, tiled=True)
    wave_field = jnp.zeros((local_comps, TROWS * NY), jnp.float32).at[:, sea_cell].set(received)
    wave_field = wave_field.reshape(local_comps, TROWS, NY)
    sea_mask = jnp.zeros((TROWS * NY,), jnp.float32).at[sea_cell].set(1.0).reshape(TROWS, NY)
    courant_x, courant_y = courant(angles, angular)
    courant_x = courant_x[:, None, None]
    courant_y = courant_y[:, None, None]
    for substep in range(ADV_STEPS):
        padded = padded_2(wave_field, (("comp", 1),), 2)
        wave_field = advect(padded, courant_x, courant_y) * sea_mask
    return wave_field


def solution(mesh):
    in_specs = (P("grp", "comp"), P("comp"), P("comp"), P("comp"))
    out_specs = P("grp", "comp", None)
    return jax.shard_map(local, mesh=mesh, in_specs=in_specs, out_specs=out_specs, check_vma=False)
```

profile of v0, /device:TPU:8, one launch (start us, length us, event | category | flops | bytes accessed | tf_op | source)
XLA Modules:
  0.0 125.3 jit_solution(4279639210668831532)
XLA Ops:
  0.8 1.4 %multiply_reduce_fusion = (f32[1536]{0:T(1024)S(1)}, f32[1536]{0:T(1024)S(1)}) fusion(f32[150,1536]{1,0:T(8,128)} %param.4, f32[150]{0:T(256)S(1)} %get-tuple-element.24, f32[150]{0:T(256)S(1)} %get-tuple-element.23), kind=kLoop, calls=%fused_computation.54 | loop fusion | flops 918528 | bytes 935088 | tf_op jit(solution)/shard_map/reduce_sum | solution.py:109
  2.2 16.9 %all-reduce = (f32[1536]{0:T(1024)S(1)}, f32[1536]{0:T(1024)S(1)}) all-reduce(f32[1536]{0:T(1024)S(1)} %get-tuple-element.6, f32[1536]{0:T(1024)S(1)} %get-tuple-element.5), channel_id=1, replica_groups=mesh['grp'=4,'comp'=128] {'grp'}, use_global_device_ids=true, to_apply=%region_1.2 | all-reduce | flops 3072 | bytes 24576 | tf_op jit(solution)/shard_map/psum | solution.py:110
  19.2 4.2 %fusion.24 = f32[150,1536]{1,0:T(8,128)S(1)} fusion(f32[150,1536]{1,0:T(8,128)S(1)} %copy-done, f32[1536]{0:T(1024)S(1)} %get-tuple-element.9, f32[1536]{0:T(1024)S(1)} %get-tuple-element.10, f32[150]{0:T(256)S(1)} %get-tuple-element.32, f32[1536]{0:T(1024)} %param.6, f32[150]{0:T(256)S(1)} %get-tuple-element.31, f32[1536]{0:T(1024)S(1)} %broadcast_multiply_fusion), kind=kLoop, calls=%fused_computation.53 | loop fusion | flops 2995200 | bytes 1868976 | tf_op jit(solution)/shard_map/mul | solution.py:50
  23.4 1.6 %copy.37 = f32[150,1536]{0,1:T(8,128)} copy(f32[150,1536]{1,0:T(8,128)S(1)} %fusion.24) | data formatting | bytes 1843200 | tf_op jit(solution)/shard_map/mul | solution.py:50
  25.0 1.5 %all_to_all.8 = f32[150,128,12]{0,2,1:T(8,128)S(1)} reshape(f32[150,1536]{0,1:T(8,128)} %copy.37) | data formatting | bytes 1843200 | tf_op jit(solution)/shard_map/all_to_all | solution.py:120
  26.4 3.5 %reshape.121 = f32[128,1,1800]{2,1,0:T(1,128)} reshape(f32[128,12,150]{2,1,0:T(8,128)S(1)} %bitcast.14) | data formatting | bytes 1843200
  30.0 17.5 %all-to-all-start = ((f32[128,1,1800]{2,1,0:T(1,128)}), f32[128,1,1800]{2,1,0:T(1,128)S(1)}, u32[]{:S(2)}, u32[]{:S(2)}) async-start(f32[128,1,1800]{2,1,0:T(1,128)} %reshape.121), calls=%async_computation | async-start | bytes 1966080 | tf_op jit(solution)/shard_map/all_to_all | solution.py:120
  47.5 6.4 %scatter_custom_fusion.1 = f32[2048]{0:T(1024)S(1)} fusion(s32[1536]{0:T(1024)S(1)} %compare_select_fusion, f32[1536]{0:T(1024)S(1)} %broadcast.447, f32[]{:T(128)} %constant.24.clone.1), kind=kCustom, calls=%fused_computation.59 | custom fusion | bytes 8196 | tf_op jit(solution)/shard_map/scatter | solution.py:123
  54.1 23.4 %all-to-all-done = f32[128,1,1800]{2,1,0:T(1,128)S(1)} async-done(((f32[128,1,1800]{2,1,0:T(1,128)}), f32[128,1,1800]{2,1,0:T(1,128)S(1)}, u32[]{:S(2)}, u32[]{:S(2)}) %all-to-all-start) | async-done | bytes 921632 | tf_op jit(solution)/shard_map/all_to_all | solution.py:120
  78.0 3.0 %reduce = f32[128,1800]{1,0:T(8,128)S(1)} reduce(f32[128,1,1800]{2,1,0:T(1,128)S(1)} %all-to-all-done, f32[]{:T(128)} %broadcast.467), dimensions={1}, to_apply=%all_to_all.9.reduce_sub_computation | reduce | bytes 1843204 | tf_op jit(solution)/shard_map/all_to_all | solution.py:120
  81.0 2.1 %reshape.122 = f32[128,12,150]{2,1,0:T(8,128)S(1)} reshape(f32[128,1800]{1,0:T(8,128)S(1)} %reduce) | data formatting | bytes 1843200
  83.1 1.3 %reshape.100 = f32[150,1536]{0,1:T(8,128)} reshape(f32[150,128,12]{0,2,1:T(8,128)S(1)} %bitcast.15) | data formatting | bytes 1843200 | tf_op jit(solution)/shard_map/all_to_all | solution.py:120
  84.5 8.0 %scatter_custom_fusion = f32[150,2048]{0,1:T(8,128)S(1)} fusion(s32[1536]{0:T(1024)S(1)} %compare_select_fusion, f32[150,1536]{0,1:T(8,128)} %reshape.100, f32[]{:T(128)} %constant.24.clone.1), kind=kCustom, calls=%fused_computation.2 | custom fusion | bytes 2150404 | tf_op jit(solution)/shard_map/scatter | solution.py:121
  94.4 1.9 %collective-permute-start = (f32[150,2,256]{2,0,1:T(8,128)S(1)}, f32[150,2,256]{2,0,1:T(8,128)S(1)}, u32[]{:S(2)}, u32[]{:S(2)}) collective-permute-start(f32[150,2,256]{2,0,1:T(8,128)S(1)} %get-tuple-element.21), channel_id=1, source_target_pairs={{0,1},{1,2},{2,3},{3,4},{4,5},{5,6},{6,7},{7,8},{8,9},{9,10},{10,1... | collective-permute-start | bytes 921608 | tf_op jit(solution)/shard_map/ppermute | solution.py:21
  96.3 5.8 %collective-permute-start.1 = (f32[150,2,256]{2,0,1:T(8,128)S(1)}, f32[150,2,256]{2,0,1:T(8,128)S(1)}, u32[]{:S(2)}, u32[]{:S(2)}) collective-permute-start(f32[150,2,256]{2,0,1:T(8,128)S(1)} %get-tuple-element.22), channel_id=1, source_target_pairs={{1,0},{2,1},{3,2},{4,3},{5,4},{6,5},{7,6},{8,7},{9,8},{10,9},{11,1... | collective-permute-start | bytes 921608 | tf_op jit(solution)/shard_map/ppermute | solution.py:24
  102.1 1.2 add_multiply_fusion.3
  104.7 1.8 %collective-permute-done.1 = f32[150,2,256]{2,0,1:T(8,128)S(1)} collective-permute-done((f32[150,2,256]{2,0,1:T(8,128)S(1)}, f32[150,2,256]{2,0,1:T(8,128)S(1)}, u32[]{:S(2)}, u32[]{:S(2)}) %collective-permute-start.1) | collective-permute-done | bytes 307232 | tf_op jit(solution)/shard_map/ppermute | solution.py:24
  106.5 1.5 %add_multiply_fusion.1 = f32[150,9,256]{2,0,1:T(8,128)S(1)} fusion(f32[150,2,256]{2,0,1:T(8,128)S(1)} %collective-permute-done.1, f32[150,8,256]{2,0,1:T(8,128)S(1)} %copy.42, f32[150,2,256]{2,0,1:T(8,128)S(1)} %collective-permute-done, f32[150]{0:T(256)S(1)} %get-tuple-element.27, f32[150]{0:T(256)S(1)} %get-tuple-element.28, ...), kind=kLoop, calls=%fused_computation.27 | loop fusion | flops 8985600 | bytes 3226950 | tf_op jit(solution)/shard_map/mul | solution.py:72
  109.6 1.9 %collective-permute-start.2 = (f32[150,2,256]{2,0,1:T(8,128)S(1)}, f32[150,2,256]{2,0,1:T(8,128)S(1)}, u32[]{:S(2)}, u32[]{:S(2)}) collective-permute-start(f32[150,2,256]{2,0,1:T(8,128)S(1)} %get-tuple-element.15), channel_id=1, source_target_pairs={{0,1},{1,2},{2,3},{3,4},{4,5},{5,6},{6,7},{7,8},{8,9},{9,10},{10,1... | collective-permute-start | bytes 921608 | tf_op jit(solution)/shard_map/ppermute | solution.py:21
  111.5 6.1 %collective-permute-start.3 = (f32[150,2,256]{2,0,1:T(8,128)S(1)}, f32[150,2,256]{2,0,1:T(8,128)S(1)}, u32[]{:S(2)}, u32[]{:S(2)}) collective-permute-start(f32[150,2,256]{2,0,1:T(8,128)S(1)} %get-tuple-element.16), channel_id=1, source_target_pairs={{1,0},{2,1},{3,2},{4,3},{5,4},{6,5},{7,6},{8,7},{9,8},{10,9},{11,1... | collective-permute-start | bytes 921608 | tf_op jit(solution)/shard_map/ppermute | solution.py:24
  117.7 1.2 add_multiply_fusion.2
  120.1 1.8 %collective-permute-done.3 = f32[150,2,256]{2,0,1:T(8,128)S(1)} collective-permute-done((f32[150,2,256]{2,0,1:T(8,128)S(1)}, f32[150,2,256]{2,0,1:T(8,128)S(1)}, u32[]{:S(2)}, u32[]{:S(2)}) %collective-permute-start.3) | collective-permute-done | bytes 307232 | tf_op jit(solution)/shard_map/ppermute | solution.py:24
  121.9 1.5 %add_multiply_fusion = f32[150,9,256]{2,0,1:T(8,128)S(1)} fusion(f32[150,2,256]{2,0,1:T(8,128)S(1)} %collective-permute-done.3, f32[150,8,256]{2,0,1:T(8,128)S(1)} %fusion.17, f32[150,2,256]{2,0,1:T(8,128)S(1)} %collective-permute-done.2, f32[150]{0:T(256)S(1)} %get-tuple-element.27, f32[150]{0:T(256)S(1)} %get-tuple-element.28, ...), kind=kLoop, calls=%fused_computation.26 | loop fusion | flops 8985600 | bytes 3226950 | tf_op jit(solution)/shard_map/mul | solution.py:72
  123.9 1.4 %copy.53 = f32[150,8,256]{2,1,0:T(8,128)} copy(f32[150,8,256]{2,0,1:T(8,128)S(1)} %fusion.14) | data formatting | bytes 2457600 | tf_op jit(solution)/shard_map/mul | solution.py:129
  (32 shorter events, 8.1 us)
Async XLA Ops:
  0.0 19.2 %copy-start = (f32[150,1536]{1,0:T(8,128)S(1)}, f32[150,1536]{1,0:T(8,128)}, u32[]{:S(2)}) copy-start(f32[150,1536]{1,0:T(8,128)} %param.4) | copy-start | bytes 2764804
  30.0 17.5 %copy-start.1 = (s32[1536]{0:T(1024)S(1)}, s32[1536]{0:T(1024)}, u32[]{:S(2)}) copy-start(s32[1536]{0:T(1024)} %param.7) | copy-start | bytes 18436
  30.0 47.5 %all-to-all-start = ((f32[128,1,1800]{2,1,0:T(1,128)}), f32[128,1,1800]{2,1,0:T(1,128)S(1)}, u32[]{:S(2)}, u32[]{:S(2)}) async-start(f32[128,1,1800]{2,1,0:T(1,128)} %reshape.121), calls=%async_computation | async-start | bytes 1966080 | tf_op jit(solution)/shard_map/all_to_all | solution.py:120
  94.4 10.3 %collective-permute-start = (f32[150,2,256]{2,0,1:T(8,128)S(1)}, f32[150,2,256]{2,0,1:T(8,128)S(1)}, u32[]{:S(2)}, u32[]{:S(2)}) collective-permute-start(f32[150,2,256]{2,0,1:T(8,128)S(1)} %get-tuple-element.21), channel_id=1, source_target_pairs={{0,1},{1,2},{2,3},{3,4},{4,5},{5,6},{6,7},{7,8},{8,9},{9,10},{10,1... | collective-permute-start | bytes 921608 | tf_op jit(solution)/shard_map/ppermute | solution.py:21
  96.3 10.2 %collective-permute-start.1 = (f32[150,2,256]{2,0,1:T(8,128)S(1)}, f32[150,2,256]{2,0,1:T(8,128)S(1)}, u32[]{:S(2)}, u32[]{:S(2)}) collective-permute-start(f32[150,2,256]{2,0,1:T(8,128)S(1)} %get-tuple-element.22), channel_id=1, source_target_pairs={{1,0},{2,1},{3,2},{4,3},{5,4},{6,5},{7,6},{8,7},{9,8},{10,9},{11,1... | collective-permute-start | bytes 921608 | tf_op jit(solution)/shard_map/ppermute | solution.py:24
  109.6 10.5 %collective-permute-start.2 = (f32[150,2,256]{2,0,1:T(8,128)S(1)}, f32[150,2,256]{2,0,1:T(8,128)S(1)}, u32[]{:S(2)}, u32[]{:S(2)}) collective-permute-start(f32[150,2,256]{2,0,1:T(8,128)S(1)} %get-tuple-element.15), channel_id=1, source_target_pairs={{0,1},{1,2},{2,3},{3,4},{4,5},{5,6},{6,7},{7,8},{8,9},{9,10},{10,1... | collective-permute-start | bytes 921608 | tf_op jit(solution)/shard_map/ppermute | solution.py:21
  111.5 10.3 %collective-permute-start.3 = (f32[150,2,256]{2,0,1:T(8,128)S(1)}, f32[150,2,256]{2,0,1:T(8,128)S(1)}, u32[]{:S(2)}, u32[]{:S(2)}) collective-permute-start(f32[150,2,256]{2,0,1:T(8,128)S(1)} %get-tuple-element.16), channel_id=1, source_target_pairs={{1,0},{2,1},{3,2},{4,3},{5,4},{6,5},{7,6},{8,7},{9,8},{10,9},{11,1... | collective-permute-start | bytes 921608 | tf_op jit(solution)/shard_map/ppermute | solution.py:24
where the time goes:
time: 126 us; the launch traced here: 125 us
  starting transfers between devices  33.2 us (26%)
  local copies, waits for them, and re-layouts  29.8 us (24%)
  waiting for transfers between devices  29.1 us (23%)
  blocking collectives  16.9 us (13%)
  other arithmetic  16.1 us (13%)
    all_to_all x1, waiting for transfers between devices, local(): lax.all_to_all(sourced, 'comp', split_axis=1, concat_axis=1, tiled=True)  23.4 us
    all_to_all x1, starting transfers between devices, local(): lax.all_to_all(sourced, 'comp', split_axis=1, concat_axis=1, tiled=True)  17.5 us
    psum x1, blocking collectives, local(): energy, inverse = lax.psum((partial_energy, partial_inverse), 'grp')  16.9 us
    ppermute x2, starting transfers between devices, padded_2(): lax.ppermute(lax.slice_in_dim(block, 0, width, axis=dim), axis, backward)  11.9 us
    scatter x1, local copies, waits for them, and re-layouts, local(): jnp.zeros((local_comps, TROWS * NY), jnp.float32).at[:, sea_cell]  7.98 us
    scatter x1, local copies, waits for them, and re-layouts, local(): jnp.zeros((TROWS * NY,), jnp.float32).at[sea_cell].set(1.0)  6.36 us
    unnamed x6, local copies, waits for them, and re-layouts  5.64 us
    mul x4, other arithmetic, face_flux(): number * (upstream + 0.5 * (1.0 - jnp.abs(number)) * koren_slope(slope_ba...  5.49 us
  transfers between devices with their start and end apart: 5, of which 5 were waited for; matrix products, arithmetic and copies ran while one was open for 8% of the time, Pallas kernels for 0%

commit v1 on v0

--- a/solution.py
+++ b/solution.py
@@ -1,3 +1,4 @@
+import functools
 import math
 import jax
 import jax.numpy as jnp
@@ -11,6 +12,16 @@
 GRAV = 9.81
 LOW_FREQ = 0.0418
 FREQ_STEP = 1.1
+
+
+def sizes_recast(vals, where_dim, along_dim):
+    new = jax.lax.axis_size("comp")
+    even = jnp.split(vals, new, axis=where_dim)
+    value_now = jax.lax.all_to_all(jnp.stack(even), "comp", 0, 0)
+    return jnp.concatenate(value_now, axis=along_dim)
+
+
+wires_get = functools.partial(sizes_recast, where_dim=1, along_dim=1)
 
 
 def padded_2(block, sides, width):
@@ -117,7 +128,7 @@
         wind_speed[None, :],
         wind_dir[None, :],
     )
-    received = lax.all_to_all(sourced, "comp", split_axis=1, concat_axis=1, tiled=True)
+    received = wires_get(sourced)
     wave_field = jnp.zeros((local_comps, TROWS * NY), jnp.float32).at[:, sea_cell].set(received)
     wave_field = wave_field.reshape(local_comps, TROWS, NY)
     sea_mask = jnp.zeros((TROWS * NY,), jnp.float32).at[sea_cell].set(1.0).reshape(TROWS, NY)

time: 126 us -> 129 us (1.024)
  local copies, waits for them, and re-layouts: 29.8 us -> 32.2 us
    unnamed x6 -> x138, local copies, waits for them, and re-layouts: 5.64 us -> 9.34 us
    reshape x0 -> x2, local copies, waits for them, and re-layouts: none -> 3.09 us  [sizes_recast(): return jnp.concatenate(value_now, axis=along_dim)]
    all_to_all x3 -> x1, local copies, waits for them, and re-layouts: 3.3 us -> 0.51 us  [sizes_recast(): value_now = jax.lax.all_to_all(jnp.stack(even), 'comp', 0, 0)]
    mul x1, other arithmetic: 4.18 us -> 6.21 us  [source_terms(): return spectra * jnp.exp(rate_in - rate_out)]
    mul x1 -> x0, local copies, waits for them, and re-layouts: 1.63 us -> none  [source_terms(): return spectra * jnp.exp(rate_in - rate_out)]
  transfers between devices with their start and end apart: 5 -> 5, of which waited for: 5 -> 5; matrix products, arithmetic and copies ran while one was open for 8% -> 7% of each run, Pallas kernels for 0% -> 0%
where the time goes in v1:
time: 129 us
  starting transfers between devices  33.1 us (26%)
  local copies, waits for them, and re-layouts  32.2 us (25%)
  waiting for transfers between devices  29.3 us (23%)
  blocking collectives  16.9 us (13%)
  other arithmetic  16.1 us (12%)
  between operations  1.3 us (1%)
    all_to_all x1, waiting for transfers between devices, sizes_recast(): value_now = jax.lax.all_to_all(jnp.stack(even), 'comp', 0, 0)  23.4 us
    all_to_all x1, starting transfers between devices, sizes_recast(): value_now = jax.lax.all_to_all(jnp.stack(even), 'comp', 0, 0)  17.4 us
    psum x1, blocking collectives, local(): energy, inverse = lax.psum((partial_energy, partial_inverse), 'grp')  16.9 us
    ppermute x2, starting transfers between devices, padded_2(): lax.ppermute(lax.slice_in_dim(block, 0, width, axis=dim), axis, backward)  11.7 us
    unnamed x138, local copies, waits for them, and re-layouts  9.34 us
    scatter x1, local copies, waits for them, and re-layouts, local(): jnp.zeros((local_comps, TROWS * NY), jnp.float32).at[:, sea_cell]  7.98 us
    scatter x1, local copies, waits for them, and re-layouts, local(): jnp.zeros((TROWS * NY,), jnp.float32).at[sea_cell].set(1.0)  6.36 us
    mul x1, other arithmetic, source_terms(): return spectra * jnp.exp(rate_in - rate_out)  6.21 us
  transfers between devices with their start and end apart: 5, of which 5 were waited for; matrix products, arithmetic and copies ran while one was open for 7% of the time, Pallas kernels for 0%

profile of v1, /device:TPU:8, one launch (start us, length us, event | category | flops | bytes accessed | tf_op | source)
XLA Modules:
  0.0 128.9 jit_solution(4983896134819390199)
XLA Ops:
  0.1 1.7 %copy.327 = f32[150,1536]{0,1:T(8,128)S(1)} copy(f32[150,1536]{1,0:T(8,128)} %param.4) | data formatting | bytes 1843200 | tf_op args[0]
  2.0 16.9 %all-reduce = (f32[1536]{0:T(1024)S(1)}, f32[1536]{0:T(1024)S(1)}) all-reduce(f32[1536]{0:T(1024)S(1)} %get-tuple-element.6, f32[1536]{0:T(1024)S(1)} %get-tuple-element.5), channel_id=1, replica_groups=mesh['grp'=4,'comp'=128] {'grp'}, use_global_device_ids=true, to_apply=%region_1.2 | all-reduce | flops 3072 | bytes 24576 | tf_op jit(solution)/shard_map/psum | solution.py:121
  19.0 6.2 %fusion.3 = f32[150,1536]{0,1:T(8,128)S(1)} fusion(f32[150,1536]{0,1:T(8,128)S(1)} %copy.327, f32[1536]{0:T(1024)S(1)} %get-tuple-element.9, f32[1536]{0:T(1024)S(1)} %get-tuple-element.10, f32[150]{0:T(256)S(1)} %get-tuple-element.32, f32[1536]{0:T(1024)S(1)} %copy-done.1, f32[150]{0:T(256)S(1)} %get-tuple-element.31, f32[1536]{0:T(1024)S(1)} %broadcast_multiply_fusion), kind=kLoop, calls=%fused_computation.6 | loop fusion | flops 2995200 | bytes 1868976 | tf_op jit(solution)/shard_map/mul | solution.py:61
  26.8 3.5 %reshape.127 = f32[128,1,1800]{2,1,0:T(1,128)} reshape(f32[128,12,150]{2,1,0:T(8,128)S(1)} %bitcast.528) | data formatting | bytes 1843200
  30.4 17.4 %all-to-all-start = ((f32[128,1,1800]{2,1,0:T(1,128)}), f32[128,1,1800]{2,1,0:T(1,128)S(1)}, u32[]{:S(2)}, u32[]{:S(2)}) async-start(f32[128,1,1800]{2,1,0:T(1,128)} %reshape.127), calls=%async_computation | async-start | bytes 1966080 | tf_op jit(solution)/shard_map/all_to_all | solution.py:20
  47.8 6.4 %scatter_custom_fusion.1 = f32[2048]{0:T(1024)S(1)} fusion(s32[1536]{0:T(1024)S(1)} %compare_select_fusion, f32[1536]{0:T(1024)S(1)} %broadcast.447, f32[]{:T(128)} %constant.24.clone.1), kind=kCustom, calls=%fused_computation.315 | custom fusion | bytes 8196 | tf_op jit(solution)/shard_map/scatter | solution.py:134
  54.3 23.4 %all-to-all-done = f32[128,1,1800]{2,1,0:T(1,128)S(1)} async-done(((f32[128,1,1800]{2,1,0:T(1,128)}), f32[128,1,1800]{2,1,0:T(1,128)S(1)}, u32[]{:S(2)}, u32[]{:S(2)}) %all-to-all-start) | async-done | bytes 921632 | tf_op jit(solution)/shard_map/all_to_all | solution.py:20
  78.3 3.0 %reduce = f32[128,1800]{1,0:T(8,128)S(1)} reduce(f32[128,1,1800]{2,1,0:T(1,128)S(1)} %all-to-all-done, f32[]{:T(128)} %broadcast.467), dimensions={1}, to_apply=%all_to_all.3.reduce_sub_computation | reduce | bytes 1843204 | tf_op jit(solution)/shard_map/all_to_all | solution.py:20
  81.3 3.5 %reshape.128 = f32[128,12,150]{2,1,0:T(8,128)} reshape(f32[128,1800]{1,0:T(8,128)S(1)} %reduce) | data formatting | bytes 1843200
  84.7 1.8 %bitcast_bitcast_fusion = f32[150,128,12]{0,2,1:T(8,128)S(1)} fusion(f32[128,12,150]{2,1,0:T(8,128)} %reshape.128), kind=kLoop, calls=%fused_computation.347 | loop fusion | bytes 1843200 | tf_op jit(solution)/shard_map/reshape | solution.py:21
  86.5 1.3 %reshape.106 = f32[150,1536]{0,1:T(8,128)} reshape(f32[150,128,12]{0,2,1:T(8,128)S(1)} %bitcast_bitcast_fusion) | data formatting | bytes 1843200 | tf_op jit(solution)/shard_map/reshape | solution.py:21
  87.8 8.0 %scatter_custom_fusion = f32[150,2048]{0,1:T(8,128)S(1)} fusion(s32[1536]{0:T(1024)S(1)} %compare_select_fusion, f32[150,1536]{0,1:T(8,128)} %reshape.106, f32[]{:T(128)} %constant.24.clone.1), kind=kCustom, calls=%fused_computation.7 | custom fusion | bytes 2150404 | tf_op jit(solution)/shard_map/scatter | solution.py:132
  97.7 1.9 %collective-permute-start = (f32[150,2,256]{2,0,1:T(8,128)S(1)}, f32[150,2,256]{2,0,1:T(8,128)S(1)}, u32[]{:S(2)}, u32[]{:S(2)}) collective-permute-start(f32[150,2,256]{2,0,1:T(8,128)S(1)} %get-tuple-element.21), channel_id=1, source_target_pairs={{0,1},{1,2},{2,3},{3,4},{4,5},{5,6},{6,7},{7,8},{8,9},{9,10},{10,1... | collective-permute-start | bytes 921608 | tf_op jit(solution)/shard_map/ppermute | solution.py:32
  99.7 5.8 %collective-permute-start.1 = (f32[150,2,256]{2,0,1:T(8,128)S(1)}, f32[150,2,256]{2,0,1:T(8,128)S(1)}, u32[]{:S(2)}, u32[]{:S(2)}) collective-permute-start(f32[150,2,256]{2,0,1:T(8,128)S(1)} %get-tuple-element.22), channel_id=1, source_target_pairs={{1,0},{2,1},{3,2},{4,3},{5,4},{6,5},{7,6},{8,7},{9,8},{10,9},{11,1... | collective-permute-start | bytes 921608 | tf_op jit(solution)/shard_map/ppermute | solution.py:35
  105.4 1.2 add_multiply_fusion.3
  106.9 1.2 collective-permute-done
  108.1 1.8 %collective-permute-done.1 = f32[150,2,256]{2,0,1:T(8,128)S(1)} collective-permute-done((f32[150,2,256]{2,0,1:T(8,128)S(1)}, f32[150,2,256]{2,0,1:T(8,128)S(1)}, u32[]{:S(2)}, u32[]{:S(2)}) %collective-permute-start.1) | collective-permute-done | bytes 307232 | tf_op jit(solution)/shard_map/ppermute | solution.py:35
  109.8 1.5 %add_multiply_fusion.1 = f32[150,9,256]{2,0,1:T(8,128)S(1)} fusion(f32[150,2,256]{2,0,1:T(8,128)S(1)} %collective-permute-done.1, f32[150,8,256]{2,0,1:T(8,128)S(1)} %copy.332, f32[150,2,256]{2,0,1:T(8,128)S(1)} %collective-permute-done, f32[150]{0:T(256)S(1)} %get-tuple-element.27, f32[150]{0:T(256)S(1)} %get-tuple-element.28, ...), kind=kLoop, calls=%fused_computation.32 | loop fusion | flops 8985600 | bytes 3226950 | tf_op jit(solution)/shard_map/mul | solution.py:83
  113.0 2.1 %collective-permute-start.2 = (f32[150,2,256]{2,0,1:T(8,128)S(1)}, f32[150,2,256]{2,0,1:T(8,128)S(1)}, u32[]{:S(2)}, u32[]{:S(2)}) collective-permute-start(f32[150,2,256]{2,0,1:T(8,128)S(1)} %get-tuple-element.15), channel_id=1, source_target_pairs={{0,1},{1,2},{2,3},{3,4},{4,5},{5,6},{6,7},{7,8},{8,9},{9,10},{10,1... | collective-permute-start | bytes 921608 | tf_op jit(solution)/shard_map/ppermute | solution.py:32
  115.1 5.9 %collective-permute-start.3 = (f32[150,2,256]{2,0,1:T(8,128)S(1)}, f32[150,2,256]{2,0,1:T(8,128)S(1)}, u32[]{:S(2)}, u32[]{:S(2)}) collective-permute-start(f32[150,2,256]{2,0,1:T(8,128)S(1)} %get-tuple-element.16), channel_id=1, source_target_pairs={{1,0},{2,1},{3,2},{4,3},{5,4},{6,5},{7,6},{8,7},{9,8},{10,9},{11,1... | collective-permute-start | bytes 921608 | tf_op jit(solution)/shard_map/ppermute | solution.py:35
  121.1 1.2 add_multiply_fusion.2
  123.5 2.0 %collective-permute-done.3 = f32[150,2,256]{2,0,1:T(8,128)S(1)} collective-permute-done((f32[150,2,256]{2,0,1:T(8,128)S(1)}, f32[150,2,256]{2,0,1:T(8,128)S(1)}, u32[]{:S(2)}, u32[]{:S(2)}) %collective-permute-start.3) | collective-permute-done | bytes 307232 | tf_op jit(solution)/shard_map/ppermute | solution.py:35
  125.5 1.5 %add_multiply_fusion = f32[150,9,256]{2,0,1:T(8,128)S(1)} fusion(f32[150,2,256]{2,0,1:T(8,128)S(1)} %collective-permute-done.3, f32[150,8,256]{2,0,1:T(8,128)S(1)} %fusion.21, f32[150,2,256]{2,0,1:T(8,128)S(1)} %collective-permute-done.2, f32[150]{0:T(256)S(1)} %get-tuple-element.27, f32[150]{0:T(256)S(1)} %get-tuple-element.28, ...), kind=kLoop, calls=%fused_computation.31 | loop fusion | flops 8985600 | bytes 3226950 | tf_op jit(solution)/shard_map/mul | solution.py:83
  127.5 1.4 %copy.343 = f32[150,8,256]{2,1,0:T(8,128)} copy(f32[150,8,256]{2,0,1:T(8,128)S(1)} %fusion.18) | data formatting | bytes 2457600 | tf_op jit(solution)/shard_map/mul | solution.py:140
  (164 shorter events, 7.0 us)
Async XLA Ops:
  0.0 1.8 %copy-start = (f32[150,1536]{1,0:T(8,128)S(1)}, f32[150,1536]{1,0:T(8,128)}, u32[]{:S(2)}) copy-start(f32[150,1536]{1,0:T(8,128)} %param.4) | copy-start | bytes 2764804
  0.0 1.8 %copy-start.2 = (f32[1536]{0:T(1024)S(1)}, f32[1536]{0:T(1024)}, u32[]{:S(2)}) copy-start(f32[1536]{0:T(1024)} %param.5) | copy-start | bytes 18436
  0.0 19.0 %copy-start.1 = (f32[1536]{0:T(1024)S(1)}, f32[1536]{0:T(1024)}, u32[]{:S(2)}) copy-start(f32[1536]{0:T(1024)} %param.6) | copy-start | bytes 18436
  26.8 20.9 %copy-start.3 = (s32[1536]{0:T(1024)S(1)}, s32[1536]{0:T(1024)}, u32[]{:S(2)}) copy-start(s32[1536]{0:T(1024)} %param.7) | copy-start | bytes 18436
  30.4 47.4 %all-to-all-start = ((f32[128,1,1800]{2,1,0:T(1,128)}), f32[128,1,1800]{2,1,0:T(1,128)S(1)}, u32[]{:S(2)}, u32[]{:S(2)}) async-start(f32[128,1,1800]{2,1,0:T(1,128)} %reshape.127), calls=%async_computation | async-start | bytes 1966080 | tf_op jit(solution)/shard_map/all_to_all | solution.py:20
  97.7 10.3 %collective-permute-start = (f32[150,2,256]{2,0,1:T(8,128)S(1)}, f32[150,2,256]{2,0,1:T(8,128)S(1)}, u32[]{:S(2)}, u32[]{:S(2)}) collective-permute-start(f32[150,2,256]{2,0,1:T(8,128)S(1)} %get-tuple-element.21), channel_id=1, source_target_pairs={{0,1},{1,2},{2,3},{3,4},{4,5},{5,6},{6,7},{7,8},{8,9},{9,10},{10,1... | collective-permute-start | bytes 921608 | tf_op jit(solution)/shard_map/ppermute | solution.py:32
  99.7 10.2 %collective-permute-start.1 = (f32[150,2,256]{2,0,1:T(8,128)S(1)}, f32[150,2,256]{2,0,1:T(8,128)S(1)}, u32[]{:S(2)}, u32[]{:S(2)}) collective-permute-start(f32[150,2,256]{2,0,1:T(8,128)S(1)} %get-tuple-element.22), channel_id=1, source_target_pairs={{1,0},{2,1},{3,2},{4,3},{5,4},{6,5},{7,6},{8,7},{9,8},{10,9},{11,1... | collective-permute-start | bytes 921608 | tf_op jit(solution)/shard_map/ppermute | solution.py:35
  113.0 10.5 %collective-permute-start.2 = (f32[150,2,256]{2,0,1:T(8,128)S(1)}, f32[150,2,256]{2,0,1:T(8,128)S(1)}, u32[]{:S(2)}, u32[]{:S(2)}) collective-permute-start(f32[150,2,256]{2,0,1:T(8,128)S(1)} %get-tuple-element.15), channel_id=1, source_target_pairs={{0,1},{1,2},{2,3},{3,4},{4,5},{5,6},{6,7},{7,8},{8,9},{9,10},{10,1... | collective-permute-start | bytes 921608 | tf_op jit(solution)/shard_map/ppermute | solution.py:32
  115.1 10.3 %collective-permute-start.3 = (f32[150,2,256]{2,0,1:T(8,128)S(1)}, f32[150,2,256]{2,0,1:T(8,128)S(1)}, u32[]{:S(2)}, u32[]{:S(2)}) collective-permute-start(f32[150,2,256]{2,0,1:T(8,128)S(1)} %get-tuple-element.16), channel_id=1, source_target_pairs={{1,0},{2,1},{3,2},{4,3},{5,4},{6,5},{7,6},{8,7},{9,8},{10,9},{11,1... | collective-permute-start | bytes 921608 | tf_op jit(solution)/shard_map/ppermute | solution.py:35
